TPU v7x, 32 devices: a whole 2x2x4 slice. The times are simulated.
32 devices in a mesh: sub: 16 (over z, y, x), panel: 2 (over core).
Axes of the slice: x: 2, y: 2, z: 4, core: 2. Of those that a mesh axis runs over, the one named last changes fastest.
Arguments:
- stiffness_tiles: bfloat16 [256, 8, 128, 128], P('sub'), may hold values from -0.1875 to 0.1875
- tile_columns: int32 [256, 8], P('sub'), may hold values from 0 to 19
- tile_counts: int32 [16, 16], P('sub'), may hold values from 1 to 8, 96 in all within a row
- phi_modes: bfloat16 [32768, 2048], P('sub', 'panel'), may hold values from -1.5 to 1.5
- halo_to_right: int32 [32], P('sub'), may hold values from 0 to 15
- halo_to_left: int32 [32], P('sub'), may hold values from 0 to 15
- liner_rows: int32 [8192], P('sub'), may hold values from 0 to 2047
- liner_owner: int32 [8192, 1], P('sub'), may hold values from 0 to 15; in each aligned block of 512 rows (0 to 511, 512 to 1023, ...) at most 32 rows name the same one
- liner_slot: int32 [8192], P('sub'), may hold values from 0 to 31
Outputs:
- reduced: float32 [2048, 2048], P('sub', 'panel')
- interface_load: float32 [512, 2048], P('sub', 'panel')
Inputs may be any that keep to these rules, and one draw needn't show every extreme that they name: `tile_counts`: counts a slab's used slots; the counts of one slab sum to 96. `tile_columns`: indices into the slab's extended tiles. `liner_owner`: among the listed rows of one slab at most 32 name one owner, and in every draw some owner is named by exactly 32 rows of some slab.
All inputs are finite; a program needn't handle non-finite values.
Results may differ from a plain program's by a relative error of at most 0.0029.
Values may be sent and summed in bfloat16 or wider, within the bound.
A program may use at most 128 MiB of HBM per device.

v0:
```python
import functools

import jax
import jax.numpy as jnp
from jax import lax
from jax.experimental import pallas as pl
from jax.experimental.pallas import tpu as pltpu
from jax.sharding import PartitionSpec as P

IF_DEV = 32
LOW = 4
PARTS = 2
MESH = pl.DeviceIdType.MESH


def kernel(
    n_sub,
    n_panel,
    cols_ref,
    counts_ref,
    to_right_ref,
    to_left_ref,
    rows_ref,
    target_ref,
    tiles_hbm,
    phi_hbm,
    red_ref,
    load_ref,
    ext,
    tiles,
    onehot,
    lhs,
    kphi,
    part,
    halo_out,
    halo_in,
    s1_out,
    s1_in,
    s2_out,
    s2_in,
    z_out,
    z_in,
    local_sem,
    halo_send,
    halo_recv,
    pan_send,
    pan_recv,
    s1_send,
    s1_recv,
    s2_send,
    s2_recv,
    z_send,
    z_recv,
):
    block_rows, slots, tile, _ = tiles.shape
    halo = halo_out.shape[2]
    rows = block_rows * tile
    width = kphi.shape[2]
    high = n_sub // LOW
    mode_rows = red_ref.shape[0]
    out_rows = mode_rows + IF_DEV
    per_panel = high // n_panel
    sub = lax.axis_index("sub")
    panel = lax.axis_index("panel")
    low, my_high = lax.rem(sub, LOW), sub // LOW
    bit0, bit1 = lax.rem(low, 2), low // 2

    def order(part_of):
        swap = 1 - part_of * (1 - lax.rem(panel, 2))
        first_bit = (1 - swap) * bit0 + swap * bit1
        second_bit = (1 - swap) * bit1 + swap * bit0
        first_weight, second_weight = 1 + swap, 2 - swap
        first_peer = sub + (1 - 2 * first_bit) * first_weight
        second_peer = sub + (1 - 2 * second_bit) * second_weight
        return first_bit, second_bit, first_weight, second_weight, first_peer, second_peer

    barrier = pltpu.get_barrier_semaphore()

    def greet(place):
        pl.semaphore_signal(barrier, inc=1, device_id=place, device_id_type=MESH)

    greet({"sub": sub + 1 - 2 * bit0, "panel": panel})
    greet({"sub": sub + 2 - 4 * bit1, "panel": panel})

    @pl.when(sub > 0)
    def _():
        greet({"sub": sub - 1, "panel": panel})

    @pl.when(sub < n_sub - 1)
    def _():
        greet({"sub": sub + 1, "panel": panel})

    for step in range(1, n_panel):
        greet({"sub": sub, "panel": lax.rem(panel + step, n_panel)})
    for step in range(1, high):
        greet({"sub": lax.rem(my_high + step, high) * LOW + low, "panel": panel})

    phi_copies = [
        pltpu.make_async_copy(
            phi_hbm.at[:, :, pl.ds(c * width, width)],
            ext.at[c, pl.ds(halo, block_rows)],
            local_sem.at[c],
        )
        for c in range(PARTS)
    ]
    tile_copy = pltpu.make_async_copy(tiles_hbm, tiles, local_sem.at[PARTS])
    for copy in phi_copies:
        copy.start()
    tile_copy.start()
    for copy in phi_copies:
        copy.wait()
    for c in range(PARTS):
        for i in range(halo):
            halo_out[c, 0, i] = ext[c, halo + to_right_ref[i]]
            halo_out[c, 1, i] = ext[c, halo + to_left_ref[i]]
    ends = jnp.where(sub > 0, 1, 0) + jnp.where(sub < n_sub - 1, 1, 0)
    pl.semaphore_wait(barrier, 2 + (n_panel - 1) + (high - 1) + ends)

    def halo_copy(c, side):
        return pltpu.make_async_remote_copy(
            src_ref=halo_out.at[c, side],
            dst_ref=halo_in.at[c, side],
            send_sem=halo_send.at[c, side],
            recv_sem=halo_recv.at[c, side],
            device_id={"sub": sub + 1 - 2 * side, "panel": panel},
            device_id_type=MESH,
        )

    def send_halo(c):
        @pl.when(sub < n_sub - 1)
        def _():
            halo_copy(c, 0).start()

        @pl.when(sub > 0)
        def _():
            halo_copy(c, 1).start()

    send_halo(0)

    def transposed(b, carry):
        for q in range(per_panel * LOW):
            lhs[
                panel * per_panel + q // LOW,
                q % LOW,
                pl.ds(0, mode_rows),
                pl.ds(pl.multiple_of(b * tile, tile), tile),
            ] = jnp.transpose(
                ext[
                    q * mode_rows // width,
                    halo + b,
                    :,
                    pl.ds(q * mode_rows % width, mode_rows),
                ]
            )
        return carry

    lax.fori_loop(0, block_rows, transposed, 0)

    def panel_copy(step, owner):
        block = lhs.at[
            pl.ds(owner * per_panel, per_panel), :, pl.ds(0, mode_rows), :
        ]
        return pltpu.make_async_remote_copy(
            src_ref=block,
            dst_ref=block,
            send_sem=pan_send.at[step],
            recv_sem=pan_recv.at[step],
            device_id={"sub": sub, "panel": lax.rem(panel + step, n_panel)},
            device_id_type=MESH,
        )

    for step in range(1, n_panel):
        panel_copy(step, panel).start()

    listed = rows_ref.shape[1]
    onehot[...] = (
        lax.broadcasted_iota(jnp.int32, (rows, listed), 0) == rows_ref[...]
    ).astype(jnp.float32).astype(jnp.bfloat16)
    wanted = LOW * IF_DEV

    def select(h, carry):
        place = lax.broadcasted_iota(jnp.int32, (wanted, listed), 0) + h * wanted
        hit = (place == target_ref[...]).astype(jnp.float32).astype(jnp.bfloat16)
        found = lax.dot_general(
            hit,
            onehot[...],
            (((1,), (1,)), ((), ())),
            preferred_element_type=jnp.float32,
        ).astype(jnp.bfloat16)
        for q in range(LOW):
            lhs[h, q, pl.ds(mode_rows, IF_DEV), :] = found[
                q * IF_DEV : (q + 1) * IF_DEV
            ]
        return carry

    lax.fori_loop(0, high, select, 0)
    tile_copy.wait()

    def products(c):
        for side in range(2):
            there = sub > 0 if side == 0 else sub < n_sub - 1
            place = pl.ds(side * (halo + block_rows), halo)

            @pl.when(there)
            def _(side=side, place=place):
                halo_copy(c, side).wait_recv()
                ext[c, place] = halo_in[c, side]

            @pl.when(jnp.logical_not(there))
            def _(place=place):
                ext[c, place] = jnp.zeros((halo, tile, width), ext.dtype)

        if c + 1 < PARTS:
            send_halo(c + 1)

        def block_row(b, carry):
            count = counts_ref[0, b]
            left = jnp.concatenate(
                [
                    jnp.where(j < count, tiles[b, j].astype(jnp.float32), 0.0).astype(
                        jnp.bfloat16
                    )
                    for j in range(slots)
                ],
                axis=1,
            )
            right = jnp.concatenate(
                [ext[c, cols_ref[j, b]] for j in range(slots)], axis=0
            )
            kphi[c, pl.ds(pl.multiple_of(b * tile, tile), tile), :] = jnp.dot(
                left, right, preferred_element_type=jnp.float32
            ).astype(jnp.bfloat16)
            return carry

        lax.fori_loop(0, block_rows, block_row, 0)

    products(0)

    for step in range(1, n_panel):
        panel_copy(step, lax.rem(panel + n_panel - step, n_panel)).wait_recv()

    def first_copy(k):
        return pltpu.make_async_remote_copy(
            src_ref=s1_out.at[k],
            dst_ref=s1_in.at[k],
            send_sem=s1_send.at[k],
            recv_sem=s1_recv.at[k],
            device_id={"sub": order(k // high)[4], "panel": panel},
            device_id_type=MESH,
        )

    def second_copy(k):
        return pltpu.make_async_remote_copy(
            src_ref=s2_out.at[k],
            dst_ref=s2_in.at[k],
            send_sem=s2_send.at[k],
            recv_sem=s2_recv.at[k],
            device_id={"sub": order(k // high)[5], "panel": panel},
            device_id_type=MESH,
        )

    def third_copy(k, slot):
        return pltpu.make_async_remote_copy(
            src_ref=z_out.at[k],
            dst_ref=z_in.at[slot],
            send_sem=z_send.at[k],
            recv_sem=z_recv.at[slot],
            device_id={
                "sub": lax.rem(my_high + 1 + lax.rem(k, high), high) * LOW + low,
                "panel": panel,
            },
            device_id_type=MESH,
        )

    chunk = min(256, width)

    total_steps = PARTS * high
    lag = 3

    def step_of(t, carry):
        for c in range(1, PARTS):

            @pl.when(t == c * high)
            def _(c=c):
                products(c)

        @pl.when(t < total_steps)
        def _():
            c = t // high
            h = lax.rem(my_high + 1 + lax.rem(t, high), high)
            first_bit, _, first_weight, second_weight, _, _ = order(c)

            def columns(i, inner):
                at = pl.ds(pl.multiple_of(i * chunk, chunk), chunk)
                product = jnp.dot(
                    lhs[h].reshape(LOW * out_rows, rows),
                    kphi[c, :, at],
                    preferred_element_type=jnp.float32,
                )
                part[t, :, :, at] = product.reshape(LOW, out_rows, chunk)
                return inner

            lax.fori_loop(0, width // chunk, columns, 0)
            for j in range(2):
                q = (1 - first_bit) * first_weight + j * second_weight
                s1_out[t, j] = part[t, q].astype(jnp.bfloat16)
            first_copy(t).start()

        @pl.when((t >= lag) & (t < total_steps + lag))
        def _():
            k = t - lag
            first_bit, second_bit, first_weight, second_weight, _, _ = order(k // high)
            first_copy(k).wait_recv()
            q = first_bit * first_weight + (1 - second_bit) * second_weight
            s2_out[k] = (
                part[k, q] + s1_in[k, 1 - second_bit].astype(jnp.float32)
            ).astype(jnp.bfloat16)
            second_copy(k).start()

        @pl.when(t >= lag + 1)
        def _():
            k = t - lag - 1
            _, second_bit, _, _, _, _ = order(k // high)
            second_copy(k).wait_recv()
            total = (
                part[k, low]
                + s1_in[k, second_bit].astype(jnp.float32)
                + s2_in[k].astype(jnp.float32)
            )

            @pl.when(lax.rem(k, high) < high - 1)
            def _():
                z_out[k] = total.astype(jnp.bfloat16)
                third_copy(k, k // high * high + my_high).start()

            for c in range(PARTS):

                @pl.when(k == (c + 1) * high - 1)
                def _(c=c):
                    red_ref[:, pl.ds(c * width, width)] = total[:mode_rows]
                    load_ref[:, pl.ds(c * width, width)] = total[mode_rows:]

        return carry

    lax.fori_loop(0, total_steps + lag + 1, step_of, 0)

    for c in range(PARTS):
        at_part = pl.ds(c * width, width)

        def gathered(k, carry, c=c, at_part=at_part):
            slot = c * high + lax.rem(my_high + 1 + k, high)
            third_copy(c * high + k, slot).wait_recv()
            value = z_in[slot].astype(jnp.float32)
            red_ref[:, at_part] += value[:mode_rows]
            load_ref[:, at_part] += value[mode_rows:]
            third_copy(c * high + k, slot).wait_send()
            return carry

        lax.fori_loop(0, high - 1, gathered, 0)

    def drained(k, carry):
        first_copy(k).wait_send()
        second_copy(k).wait_send()
        return carry

    lax.fori_loop(0, total_steps, drained, 0)
    for step in range(1, n_panel):
        panel_copy(step, panel).wait_send()

    for c in range(PARTS):

        @pl.when(sub < n_sub - 1)
        def _(c=c):
            halo_copy(c, 0).wait_send()

        @pl.when(sub > 0)
        def _(c=c):
            halo_copy(c, 1).wait_send()


def body(
    n_sub,
    n_panel,
    stiffness_tiles,
    tile_columns,
    tile_counts,
    phi_modes,
    halo_to_right,
    halo_to_left,
    liner_rows,
    liner_owner,
    liner_slot,
):
    block_rows, slots, tile, _ = stiffness_tiles.shape
    rows, width = phi_modes.shape
    high = n_sub // LOW
    mode_rows = width * n_panel // n_sub
    out_rows = mode_rows + IF_DEV
    halo = halo_to_right.shape[0]
    half = width // PARTS
    listed = liner_rows.shape[0]
    target = (liner_owner[:, 0] * IF_DEV + liner_slot).reshape(1, listed)
    bf16, f32 = jnp.bfloat16, jnp.float32
    smem = pl.BlockSpec(memory_space=pltpu.SMEM)
    vmem = pl.BlockSpec(memory_space=pltpu.VMEM)
    hbm = pl.BlockSpec(memory_space=pl.ANY)
    dma = pltpu.SemaphoreType.DMA
    return pl.pallas_call(
        functools.partial(kernel, n_sub, n_panel),
        out_shape=(
            jax.ShapeDtypeStruct((mode_rows, width), f32),
            jax.ShapeDtypeStruct((IF_DEV, width), f32),
        ),
        in_specs=[smem, smem, smem, smem, vmem, vmem, hbm, hbm],
        out_specs=(vmem, vmem),
        scratch_shapes=[
            pltpu.VMEM((PARTS, block_rows + 2 * halo, tile, half), bf16),
            pltpu.VMEM((block_rows, slots, tile, tile), bf16),
            pltpu.VMEM((rows, listed), bf16),
            pltpu.VMEM((high, LOW, out_rows, rows), bf16),
            pltpu.VMEM((PARTS, rows, half), bf16),
            pltpu.VMEM((PARTS * high, LOW, out_rows, half), f32),
            pltpu.VMEM((PARTS, 2, halo, tile, half), bf16),
            pltpu.VMEM((PARTS, 2, halo, tile, half), bf16),
            pltpu.VMEM((PARTS * high, 2, out_rows, half), bf16),
            pltpu.VMEM((PARTS * high, 2, out_rows, half), bf16),
            pltpu.VMEM((PARTS * high, out_rows, half), bf16),
            pltpu.VMEM((PARTS * high, out_rows, half), bf16),
            pltpu.VMEM((PARTS * high, out_rows, half), bf16),
            pltpu.VMEM((PARTS * high, out_rows, half), bf16),
            dma((PARTS + 1,)),
            dma((PARTS, 2)),
            dma((PARTS, 2)),
            dma((n_panel,)),
            dma((n_panel,)),
        ]
        + [dma((PARTS * high,))] * 6,
        compiler_params=pltpu.CompilerParams(
            collective_id=0, has_side_effects=True, vmem_limit_bytes=60 << 20
        ),
    )(
        tile_columns.T,
        tile_counts,
        halo_to_right,
        halo_to_left,
        liner_rows.reshape(1, listed),
        target,
        stiffness_tiles,
        phi_modes.reshape(block_rows, tile, width),
    )


def solution(mesh):
    return jax.shard_map(
        functools.partial(body, mesh.shape["sub"], mesh.shape["panel"]),
        mesh=mesh,
        in_specs=(
            P("sub", None, None, None),
            P("sub", None),
            P("sub", None),
            P("sub", "panel"),
            P("sub"),
            P("sub"),
            P("sub"),
            P("sub", None),
            P("sub"),
        ),
        out_specs=(P("sub", "panel"), P("sub", "panel")),
        check_vma=False,
    )
```

profile of v0, /device:TPU:10, one launch (start us, length us, event | category | flops | bytes accessed | tf_op | source)
XLA Modules:
  0.0 94.2 jit_solution(11301987054273080225)
XLA Ops:
  0.6 0.7 broadcast_multiply_fusion
  1.3 1.3 %add.3 = s32[512]{0:T(512)} add(s32[512]{0:T(512)S(1)} %bitcast.6, s32[512]{0:T(512)} %param.17) | non-fusion elementwise | flops 512 | bytes 6144 | tf_op jit(solution)/shard_map/add | solution.py:402
  2.6 88.2 %shard_map.104 = (f32[128,1024]{1,0:T(8,128)}, f32[32,1024]{1,0:T(8,128)}) custom-call(s32[8,16]{1,0:T(8,128)} %bitcast.8, s32[1,16]{1,0:T(1,128)} %counts_ref.1, s32[2]{0:T(128)} %to_right_ref.1, s32[2]{0:T(128)} %to_left_ref.1, s32[1,512]{1,0:T(1,128)} %bitcast.9, s32[1,512]{1,0:T(1,128)} %bitcast.7, bf16[16,8,128,128]{3,2,1,0:T(8,128)(2,1)} %tiles_hbm.1, ...), custom_call_target="tpu_custom_call" | custom-call | tf_op jit(solution)/shard_map/pallas_call | solution.py:408
  90.7 1.9 %copy.13 = f32[128,1024]{1,0:T(8,128)} copy(f32[128,1024]{1,0:T(8,128)} %get-tuple-element.4) | data formatting | bytes 1048576
  92.6 1.6 %copy.14 = f32[32,1024]{1,0:T(8,128)} copy(f32[32,1024]{1,0:T(8,128)} %get-tuple-element.5) | data formatting | bytes 262144
where the time goes:
time: 94.5 us; the launch traced here: 94.2 us
  Pallas kernels  88.2 us (93%)
  local copies, waits for them, and re-layouts  3.45 us (4%)
  other arithmetic  1.95 us (2%)
    pallas_call x1, Pallas kernels, body(): pl.pallas_call(functools.partial(kernel, n_sub, n_panel), out_shape=(jax....  88.2 us
    unnamed x2, local copies, waits for them, and re-layouts  3.45 us

commit v1 on v0

v1 whole, which is shorter than its diff:
```python
import functools

import jax
import jax.numpy as jnp
from jax import lax
from jax.experimental import pallas as pl
from jax.experimental.pallas import tpu as pltpu
from jax.sharding import PartitionSpec as P

IF_DEV = 32
LOW = 4
LAG = 3
CHAIN_LAG = 1
CHAIN_ROWS = 48
LONGEST_CHAIN = 4
MESH = pl.DeviceIdType.MESH


def sizes(n_sub, width, mode_rows):
    parts = max(1, min(4, width // 128))
    high = n_sub // LOW
    chain = CHAIN_ROWS if high <= LONGEST_CHAIN and mode_rows % 16 == 0 else 0
    return parts, width // parts, high, chain


def kernel(n_sub, n_panel, parts, chain, *refs):
    refs = list(refs)

    def take(count):
        taken, refs[:] = refs[:count], refs[count:]
        return taken

    cols_ref, counts_ref, to_right_ref, to_left_ref, rows_ref, owner_ref, slot_ref = take(7)
    tiles_hbm, phi_hbm, red_ref, load_ref = take(4)
    ext = take(parts)
    tiles, onehot, lhs, kphi, part, halo_out, halo_in = take(7)
    s1_out, s1_in, s2_out, s2_in, z_out, z_in = take(6)
    c_out, c_in, c1_out, c1_in, c2_out, c2_in = take(6)
    local_sem, halo_send, halo_recv, pan_send, pan_recv = take(5)
    s1_send, s1_recv, s2_send, s2_recv, z_send, z_recv = take(6)
    c_send, c_recv, c1_send, c1_recv, c2_send, c2_recv = take(6)

    block_rows, slots, tile, _ = tiles.shape
    halo = halo_out.shape[2]
    rows = block_rows * tile
    width = kphi.shape[2]
    high = n_sub // LOW
    mode_rows = red_ref.shape[0]
    out_rows = mode_rows + IF_DEV
    direct = out_rows - chain
    per_panel = high // n_panel
    total_steps = parts * high
    empty = block_rows + 2 * halo
    f32, bf16 = jnp.float32, jnp.bfloat16
    sub = lax.axis_index("sub")
    panel = lax.axis_index("panel")
    low, my_high = lax.rem(sub, LOW), sub // LOW
    bit0, bit1 = lax.rem(low, 2), low // 2
    odd = lax.rem(panel, 2)

    def order(c):
        first0 = jnp.where(c == parts - 1, 1 - odd, 0) + jnp.where(c == parts - 2, odd, 0)
        swap = 1 - first0
        first_bit = (1 - swap) * bit0 + swap * bit1
        second_bit = (1 - swap) * bit1 + swap * bit0
        first_weight, second_weight = 1 + swap, 2 - swap
        first_peer = sub + (1 - 2 * first_bit) * first_weight
        second_peer = sub + (1 - 2 * second_bit) * second_weight
        return first_bit, second_bit, first_weight, second_weight, first_peer, second_peer

    below, above = my_high, high - 1 - my_high
    nearer = jnp.minimum(below, above)
    excess = jnp.abs(above - below)
    far_way = jnp.where(above >= below, 1, -1)

    def dest(t):
        k = lax.rem(t, high)
        own_first = lax.rem(k + panel * per_panel, high)
        later = jnp.maximum(k - excess, 0)
        distance = jnp.where(k < excess, nearer + excess - k, nearer - later // 2)
        way = jnp.where((k < excess) | (lax.rem(later, 2) == 0), far_way, -far_way)
        return jnp.where(t < high, own_first, my_high + way * distance)

    barrier = pltpu.get_barrier_semaphore()

    def greet(place):
        pl.semaphore_signal(barrier, inc=1, device_id=place, device_id_type=MESH)

    greet({"sub": sub + 1 - 2 * bit0, "panel": panel})
    greet({"sub": sub + 2 - 4 * bit1, "panel": panel})

    @pl.when(sub > 0)
    def _():
        greet({"sub": sub - 1, "panel": panel})

    @pl.when(sub < n_sub - 1)
    def _():
        greet({"sub": sub + 1, "panel": panel})

    for step in range(1, n_panel):
        greet({"sub": sub, "panel": lax.rem(panel + step, n_panel)})
    for step in range(1, high):
        greet({"sub": lax.rem(my_high + step, high) * LOW + low, "panel": panel})

    phi_copies = [
        pltpu.make_async_copy(
            phi_hbm.at[:, :, pl.ds(c * width, width)],
            ext[c].at[pl.ds(halo, block_rows)],
            local_sem.at[c],
        )
        for c in range(parts)
    ]
    tile_copy = pltpu.make_async_copy(tiles_hbm, tiles, local_sem.at[parts])
    for copy in phi_copies:
        copy.start()
    tile_copy.start()

    def halo_copy(c, side):
        return pltpu.make_async_remote_copy(
            src_ref=halo_out.at[c, side],
            dst_ref=halo_in.at[c, side],
            send_sem=halo_send.at[c, side],
            recv_sem=halo_recv.at[c, side],
            device_id={"sub": sub + 1 - 2 * side, "panel": panel},
            device_id_type=MESH,
        )

    def prepare_halo(c):
        phi_copies[c].wait()
        for i in range(halo):
            halo_out[c, 0, i] = ext[c][halo + to_right_ref[i]]
            halo_out[c, 1, i] = ext[c][halo + to_left_ref[i]]

    def send_halo(c):
        @pl.when(sub < n_sub - 1)
        def _():
            halo_copy(c, 0).start()

        @pl.when(sub > 0)
        def _():
            halo_copy(c, 1).start()

    prepare_halo(0)
    ends = jnp.where(sub > 0, 1, 0) + jnp.where(sub < n_sub - 1, 1, 0)
    pl.semaphore_wait(barrier, 2 + (n_panel - 1) + (high - 1) + ends)
    send_halo(0)
    for c in range(1, parts):
        prepare_halo(c)

    def panel_copy(step, piece, owner):
        block = lhs.at[owner * per_panel + piece, :, pl.ds(0, mode_rows), :]
        return pltpu.make_async_remote_copy(
            src_ref=block,
            dst_ref=block,
            send_sem=pan_send.at[step, piece],
            recv_sem=pan_recv.at[step, piece],
            device_id={"sub": sub, "panel": lax.rem(panel + step, n_panel)},
            device_id_type=MESH,
        )

    for piece in range(per_panel):

        def transposed(b, carry, piece=piece):
            for q in range(LOW):
                at = (piece * LOW + q) * mode_rows
                lhs[
                    panel * per_panel + piece,
                    q,
                    pl.ds(0, mode_rows),
                    pl.ds(pl.multiple_of(b * tile, tile), tile),
                ] = jnp.transpose(
                    ext[at // width][halo + b, :, pl.ds(at % width, mode_rows)]
                )
            return carry

        lax.fori_loop(0, block_rows, transposed, 0)
        for step in range(1, n_panel):
            panel_copy(step, piece, panel).start()

    listed = rows_ref.shape[1]
    onehot[...] = (
        (lax.broadcasted_iota(jnp.int32, (rows, listed), 0) == rows_ref[...])
        .astype(f32)
        .astype(bf16)
    )
    target = owner_ref[...] * IF_DEV + slot_ref[...]
    wanted = LOW * IF_DEV

    def select(h, carry):
        place = lax.broadcasted_iota(jnp.int32, (wanted, listed), 0) + h * wanted
        hit = (place == target).astype(f32).astype(bf16)
        found = lax.dot_general(
            hit,
            onehot[...],
            (((1,), (1,)), ((), ())),
            preferred_element_type=f32,
        ).astype(bf16)
        for q in range(LOW):
            lhs[h, q, pl.ds(mode_rows, IF_DEV), :] = found[
                q * IF_DEV : (q + 1) * IF_DEV
            ]
        return carry

    lax.fori_loop(0, high, select, 0)
    for c in range(parts):
        ext[c][empty] = jnp.zeros((tile, width), bf16)
    tile_copy.wait()

    def products(c):
        for side in range(2):
            there = sub > 0 if side == 0 else sub < n_sub - 1
            place = pl.ds(side * (halo + block_rows), halo)

            @pl.when(there)
            def _(side=side, place=place):
                halo_copy(c, side).wait_recv()
                ext[c][place] = halo_in[c, side]

            @pl.when(jnp.logical_not(there))
            def _(place=place):
                ext[c][place] = jnp.zeros((halo, tile, width), bf16)

        if c + 1 < parts:
            send_halo(c + 1)

        def block_row(b, carry):
            count = counts_ref[0, b]
            left = jnp.concatenate([tiles[b, j] for j in range(slots)], axis=1)
            right = jnp.concatenate(
                [
                    ext[c][jnp.where(j < count, cols_ref[j, b], empty)]
                    for j in range(slots)
                ],
                axis=0,
            )
            kphi[c, pl.ds(pl.multiple_of(b * tile, tile), tile), :] = jnp.dot(
                left, right, preferred_element_type=f32
            ).astype(bf16)
            return carry

        lax.fori_loop(0, block_rows, block_row, 0, unroll=4)

    def first_copy(k):
        return pltpu.make_async_remote_copy(
            src_ref=s1_out.at[k],
            dst_ref=s1_in.at[k],
            send_sem=s1_send.at[k],
            recv_sem=s1_recv.at[k],
            device_id={"sub": order(k // high)[4], "panel": panel},
            device_id_type=MESH,
        )

    def second_copy(k):
        return pltpu.make_async_remote_copy(
            src_ref=s2_out.at[k],
            dst_ref=s2_in.at[k],
            send_sem=s2_send.at[k],
            recv_sem=s2_recv.at[k],
            device_id={"sub": order(k // high)[5], "panel": panel},
            device_id_type=MESH,
        )

    def third_copy(k, h, slot):
        return pltpu.make_async_remote_copy(
            src_ref=z_out.at[k],
            dst_ref=z_in.at[slot],
            send_sem=z_send.at[k],
            recv_sem=z_recv.at[slot],
            device_id={"sub": h * LOW + low, "panel": panel},
            device_id_type=MESH,
        )

    def chain_copy(k, next_high, slot):
        return pltpu.make_async_remote_copy(
            src_ref=c_out.at[k],
            dst_ref=c_in.at[slot],
            send_sem=c_send.at[k],
            recv_sem=c_recv.at[slot],
            device_id={"sub": next_high * LOW + low, "panel": panel},
            device_id_type=MESH,
        )

    def chain_first(c):
        return pltpu.make_async_remote_copy(
            src_ref=c1_out.at[c],
            dst_ref=c1_in.at[c],
            send_sem=c1_send.at[c],
            recv_sem=c1_recv.at[c],
            device_id={"sub": order(c)[4], "panel": panel},
            device_id_type=MESH,
        )

    def chain_second(c):
        return pltpu.make_async_remote_copy(
            src_ref=c2_out.at[c],
            dst_ref=c2_in.at[c],
            send_sem=c2_send.at[c],
            recv_sem=c2_recv.at[c],
            device_id={"sub": order(c)[5], "panel": panel},
            device_id_type=MESH,
        )

    head, tail = pl.ds(0, direct), pl.ds(direct, chain)

    def chain_add(k, slot):
        chain_copy(k, my_high, slot).wait_recv()
        part[k, :, tail, :] += c_in[slot].astype(f32)

    def chain_step(k):
        h = dest(k)
        c = k // high
        base = c * (high + 1)

        @pl.when(h != my_high)
        def _():
            up = jnp.where(h > my_high, 1, 0)

            @pl.when(jnp.where(up == 1, below, above) > 0)
            def _():
                chain_add(k, base + h)

            c_out[k] = part[k, :, tail, :].astype(bf16)
            next_high = my_high + 2 * up - 1
            slot = jnp.where((up == 0) & (next_high == h), high, h)
            chain_copy(k, next_high, base + slot).start()

        @pl.when(h == my_high)
        def _():
            @pl.when(below > 0)
            def _():
                chain_add(k, base + my_high)

            @pl.when(above > 0)
            def _():
                chain_add(k, base + high)

            first_bit, _, first_weight, second_weight, _, _ = order(c)
            for j in range(2):
                q = (1 - first_bit) * first_weight + j * second_weight
                c1_out[c, j] = part[k, q, tail, :].astype(bf16)
            chain_first(c).start()

    def chain_turn(k):
        c = k // high
        first_bit, second_bit, first_weight, second_weight, _, _ = order(c)
        chain_first(c).wait_recv()
        q = first_bit * first_weight + (1 - second_bit) * second_weight
        c2_out[c] = (
            part[k, q, tail, :] + c1_in[c, 1 - second_bit].astype(f32)
        ).astype(bf16)
        chain_second(c).start()

    def put(value, start, at):
        count = value.shape[0]
        cut = max(0, min(count, mode_rows - start))
        if cut:
            red_ref[pl.ds(start, cut), at] = value[:cut]
        if cut < count:
            load_ref[pl.ds(start + cut - mode_rows, count - cut), at] = value[cut:]

    def columns_of(c):
        return pl.ds(pl.multiple_of(c * width, width), width)

    def chain_last(k):
        c = k // high
        _, second_bit, _, _, _, _ = order(c)
        chain_second(c).wait_recv()
        put(
            part[k, low, tail, :]
            + c1_in[c, second_bit].astype(f32)
            + c2_in[c].astype(f32),
            direct,
            columns_of(c),
        )

    def step_of(t, carry):
        for c in range(parts):

            @pl.when(t == c * high)
            def _(c=c):
                products(c)

        for step in range(1, n_panel):
            for piece in range(per_panel):

                @pl.when(t == step * per_panel + piece)
                def _(step=step, piece=piece):
                    owner = lax.rem(panel + step, n_panel)
                    panel_copy(n_panel - step, piece, owner).wait_recv()

        @pl.when(t < total_steps)
        def _():
            c, h = t // high, dest(t)
            first_bit, _, first_weight, second_weight, _, _ = order(c)
            product = jnp.dot(
                lhs[h].reshape(LOW * out_rows, rows),
                kphi[c],
                preferred_element_type=f32,
            )
            part[t] = product.reshape(LOW, out_rows, width)
            for j in range(2):
                q = (1 - first_bit) * first_weight + j * second_weight
                s1_out[t, j] = part[t, q, head, :].astype(bf16)
            first_copy(t).start()

        @pl.when((t >= LAG) & (t < total_steps + LAG))
        def _():
            k = t - LAG
            first_bit, second_bit, first_weight, second_weight, _, _ = order(k // high)
            first_copy(k).wait_recv()
            q = first_bit * first_weight + (1 - second_bit) * second_weight
            s2_out[k] = (
                part[k, q, head, :] + s1_in[k, 1 - second_bit].astype(f32)
            ).astype(bf16)
            second_copy(k).start()

        @pl.when((t >= LAG + 1) & (t < total_steps + LAG + 1))
        def _():
            k = t - LAG - 1
            c, h = k // high, dest(k)
            _, second_bit, _, _, _, _ = order(c)
            second_copy(k).wait_recv()
            total = (
                part[k, low, head, :]
                + s1_in[k, second_bit].astype(f32)
                + s2_in[k].astype(f32)
            )

            @pl.when(h != my_high)
            def _():
                z_out[k] = total.astype(bf16)
                third_copy(k, h, c * high + my_high).start()

            @pl.when(h == my_high)
            def _():
                put(total, 0, columns_of(c))

        if chain:

            def hops(i, inner):
                k = t - CHAIN_LAG - i
                inside = (k >= 0) & (k < total_steps)
                h = dest(jnp.maximum(k, 0))
                behind = jnp.where(h > my_high, below, above)
                turn = jnp.where(h == my_high, high - 1, behind)

                @pl.when(inside & (turn == i))
                def _():
                    chain_step(k)

                return inner

            lax.fori_loop(0, high, hops, 0)

            for wait, action in ((2, chain_turn), (3, chain_last)):
                k = t - CHAIN_LAG - (high - 1) - wait

                @pl.when((k >= 0) & (k < total_steps) & (dest(jnp.maximum(k, 0)) == my_high))
                def _(k=k, action=action):
                    action(k)

        return carry

    last = max(LAG + 1, CHAIN_LAG + high - 1 + 3 if chain else 0)
    lax.fori_loop(0, total_steps + last, step_of, 0)

    def gathered(c, carry):
        at = columns_of(c)
        cut = min(direct, mode_rows)

        def one(i, inner):
            slot = c * high + lax.rem(my_high + 1 + i, high)
            third_copy(slot, my_high, slot).wait_recv()
            red_ref[pl.ds(0, cut), at] += z_in[slot, pl.ds(0, cut), :].astype(f32)
            if direct > mode_rows:
                extra = pl.ds(0, direct - mode_rows)
                load_ref[extra, at] += z_in[slot, pl.ds(cut, direct - cut), :].astype(f32)
            return inner

        return lax.fori_loop(0, high - 1, one, carry)

    lax.fori_loop(0, parts, gathered, 0)

    def drained(k, carry):
        first_copy(k).wait_send()
        second_copy(k).wait_send()

        @pl.when(dest(k) != my_high)
        def _():
            third_copy(k, my_high, k).wait_send()
            if chain:
                chain_copy(k, my_high, k).wait_send()

        return carry

    lax.fori_loop(0, total_steps, drained, 0)
    for c in range(parts):
        if chain:
            chain_first(c).wait_send()
            chain_second(c).wait_send()

        @pl.when(sub < n_sub - 1)
        def _(c=c):
            halo_copy(c, 0).wait_send()

        @pl.when(sub > 0)
        def _(c=c):
            halo_copy(c, 1).wait_send()

    for step in range(1, n_panel):
        for piece in range(per_panel):
            panel_copy(step, piece, panel).wait_send()


def body(
    n_sub,
    n_panel,
    stiffness_tiles,
    tile_columns,
    tile_counts,
    phi_modes,
    halo_to_right,
    halo_to_left,
    liner_rows,
    liner_owner,
    liner_slot,
):
    block_rows, slots, tile, _ = stiffness_tiles.shape
    rows, columns = phi_modes.shape
    mode_rows = columns * n_panel // n_sub
    parts, width, high, chain = sizes(n_sub, columns, mode_rows)
    out_rows = mode_rows + IF_DEV
    direct = out_rows - chain
    links = chain or 16
    halo = halo_to_right.shape[0]
    listed = liner_rows.shape[0]
    steps = parts * high
    bf16, f32 = jnp.bfloat16, jnp.float32
    smem = pl.BlockSpec(memory_space=pltpu.SMEM)
    vmem = pl.BlockSpec(memory_space=pltpu.VMEM)
    hbm = pl.BlockSpec(memory_space=pl.ANY)
    dma = pltpu.SemaphoreType.DMA
    chains = steps if chain else 1
    arrivals = parts * (high + 1) if chain else 1
    return pl.pallas_call(
        functools.partial(kernel, n_sub, n_panel, parts, chain),
        out_shape=(
            jax.ShapeDtypeStruct((mode_rows, columns), f32),
            jax.ShapeDtypeStruct((IF_DEV, columns), f32),
        ),
        in_specs=[smem, smem, smem, smem, vmem, vmem, vmem, hbm, hbm],
        out_specs=(vmem, vmem),
        scratch_shapes=[
            pltpu.VMEM((block_rows + 2 * halo + 1, tile, width), bf16)
            for _ in range(parts)
        ]
        + [
            pltpu.VMEM((block_rows, slots, tile, tile), bf16),
            pltpu.VMEM((rows, listed), bf16),
            pltpu.VMEM((high, LOW, out_rows, rows), bf16),
            pltpu.VMEM((parts, rows, width), bf16),
            pltpu.VMEM((steps, LOW, out_rows, width), f32),
            pltpu.VMEM((parts, 2, halo, tile, width), bf16),
            pltpu.VMEM((parts, 2, halo, tile, width), bf16),
            pltpu.VMEM((steps, 2, direct, width), bf16),
            pltpu.VMEM((steps, 2, direct, width), bf16),
            pltpu.VMEM((steps, direct, width), bf16),
            pltpu.VMEM((steps, direct, width), bf16),
            pltpu.VMEM((steps, direct, width), bf16),
            pltpu.VMEM((steps, direct, width), bf16),
            pltpu.VMEM((chains, LOW, links, width), bf16),
            pltpu.VMEM((arrivals, LOW, links, width), bf16),
            pltpu.VMEM((parts, 2, links, width), bf16),
            pltpu.VMEM((parts, 2, links, width), bf16),
            pltpu.VMEM((parts, links, width), bf16),
            pltpu.VMEM((parts, links, width), bf16),
            dma((parts + 1,)),
            dma((parts, 2)),
            dma((parts, 2)),
            dma((n_panel, high // n_panel)),
            dma((n_panel, high // n_panel)),
        ]
        + [dma((steps,))] * 6
        + [dma((chains,)), dma((arrivals,))]
        + [dma((parts,))] * 4,
        compiler_params=pltpu.CompilerParams(
            collective_id=0, has_side_effects=True, vmem_limit_bytes=60 << 20
        ),
    )(
        tile_columns.T,
        tile_counts,
        halo_to_right,
        halo_to_left,
        liner_rows.reshape(1, listed),
        liner_owner.reshape(1, listed),
        liner_slot.reshape(1, listed),
        stiffness_tiles,
        phi_modes.reshape(block_rows, tile, columns),
    )


def solution(mesh):
    return jax.shard_map(
        functools.partial(body, mesh.shape["sub"], mesh.shape["panel"]),
        mesh=mesh,
        in_specs=(
            P("sub", None, None, None),
            P("sub", None),
            P("sub", None),
            P("sub", "panel"),
            P("sub"),
            P("sub"),
            P("sub"),
            P("sub", None),
            P("sub"),
        ),
        out_specs=(P("sub", "panel"), P("sub", "panel")),
        check_vma=False,
    )
```

time: 94.5 us -> 93.5 us (0.989)
  the two profiles are of different devices: /device:TPU:10 before, /device:TPU:0 now
where the time goes in v1:
time: 93.5 us; the launch traced here: 93.3 us
  Pallas kernels  89.2 us (95%)
  local copies, waits for them, and re-layouts  3.45 us (4%)
    pallas_call x1, Pallas kernels, body(): pl.pallas_call(functools.partial(kernel, n_sub, n_panel, parts, chain), o...  89.2 us
    unnamed x2, local copies, waits for them, and re-layouts  3.45 us

profile of v1, /device:TPU:0, one launch (start us, length us, event | category | flops | bytes accessed | tf_op | source)
XLA Modules:
  0.0 93.3 jit_solution(13251173454119189379)
XLA Ops:
  0.6 89.2 %shard_map.104 = (f32[128,1024]{1,0:T(8,128)}, f32[32,1024]{1,0:T(8,128)}) custom-call(s32[8,16]{1,0:T(8,128)} %bitcast.6, s32[1,16]{1,0:T(1,128)} %refs_1_.1, s32[2]{0:T(128)} %refs_2_.1, s32[2]{0:T(128)} %refs_3_.1, s32[1,512]{1,0:T(1,128)} %bitcast.7, s32[1,512]{1,0:T(1,128)} %bitcast.8, s32[1,512]{1,0:T(1,128)} %bitcast.9, ...), custom_call_target="tpu_custom_call" | custom-call | tf_op jit(solution)/shard_map/pallas_call | solution.py:545
  89.8 1.9 %copy.13 = f32[128,1024]{1,0:T(8,128)} copy(f32[128,1024]{1,0:T(8,128)} %get-tuple-element.4) | data formatting | bytes 1048576
  91.7 1.6 %copy.14 = f32[32,1024]{1,0:T(8,128)} copy(f32[32,1024]{1,0:T(8,128)} %get-tuple-element.5) | data formatting | bytes 262144

commit v2 on v1

v2 whole, which is shorter than its diff:
```python
import functools

import jax
import jax.numpy as jnp
from jax import lax
from jax.experimental import pallas as pl
from jax.experimental.pallas import tpu as pltpu
from jax.sharding import PartitionSpec as P

IF_DEV = 32
LOW = 4
LAG = 3
NEXT = 5
REST = 3
TURNS = (1, 3, 6, 8)
CROSS_ROWS = 48
MESH = pl.DeviceIdType.MESH


def sizes(n_sub, n_panel, width):
    parts = max(1, min(4, width // 128))
    high = n_sub // LOW
    cross = CROSS_ROWS if high == 4 and n_panel == 2 else 0
    return parts, width // parts, high, cross


def kernel(n_sub, n_panel, parts, cross, *refs):
    refs = list(refs)

    def take(count):
        taken, refs[:] = refs[:count], refs[count:]
        return taken

    cols_ref, counts_ref, to_right_ref, to_left_ref, rows_ref, owner_ref, slot_ref = take(7)
    tiles_hbm, phi_hbm, red_ref, load_ref = take(4)
    ext = take(parts)
    tiles, hit, lhs, kphi, part, halo_out, halo_in = take(7)
    s1_out, s1_in, s2_out, s2_in, z_out, z_in = take(6)
    b1_out, b1_in, b2_out, b2_in, b3_out, b3_in, b4_out, b4_in = take(8)
    local_sem, halo_send, halo_recv, pan_send, pan_recv = take(5)
    s1_send, s1_recv, s2_send, s2_recv, z_send, z_recv = take(6)
    b1_send, b1_recv, b2_send, b2_recv, b3_send, b3_recv, b4_send, b4_recv = take(8)

    block_rows, slots, tile, _ = tiles.shape
    halo = halo_out.shape[2]
    rows = block_rows * tile
    width = kphi.shape[2]
    high = n_sub // LOW
    mode_rows = red_ref.shape[0]
    out_rows = mode_rows + IF_DEV
    direct = out_rows - cross
    per_panel = high // n_panel
    total_steps = parts * high
    empty = block_rows + 2 * halo
    f32, bf16 = jnp.float32, jnp.bfloat16
    sub = lax.axis_index("sub")
    panel = lax.axis_index("panel")
    low, my_high = lax.rem(sub, LOW), sub // LOW
    bit0, bit1 = lax.rem(low, 2), low // 2
    odd = lax.rem(panel, 2)

    def first_of(t):
        k = lax.rem(t, 4)
        turn = jnp.where(k == 1 + 2 * odd, 1, 0)
        return jnp.where(t >= total_steps - high, jnp.where(lax.rem(k, 2) == 1 - odd, 1, 0), turn)

    def order(first0):
        swap = 1 - first0
        first_bit = (1 - swap) * bit0 + swap * bit1
        second_bit = (1 - swap) * bit1 + swap * bit0
        first_weight, second_weight = 1 + swap, 2 - swap
        first_peer = sub + (1 - 2 * first_bit) * first_weight
        second_peer = sub + (1 - 2 * second_bit) * second_weight
        return first_bit, second_bit, first_weight, second_weight, first_peer, second_peer

    high0, high1 = lax.rem(my_high, 2), my_high // 2

    def flip(mask):
        mask0, mask1 = lax.rem(mask, 2), mask // 2
        return (high0 + mask0 - 2 * high0 * mask0) + 2 * (high1 + mask1 - 2 * high1 * mask1)

    def mask_of(t):
        k = lax.rem(t, high)
        apart = jnp.abs(high1 - panel)
        begin = 2 * jnp.abs(k // 2 - apart) + 1 - lax.rem(k, 2)
        later = 3 - k // 2 - 2 * lax.rem(k, 2)
        return jnp.where(t < high, begin, later)

    def dest(t):
        if cross:
            return flip(mask_of(t))
        k = lax.rem(t, high)
        return lax.rem(k + jnp.where(t < high, panel * per_panel, my_high + 1), high)

    barrier = pltpu.get_barrier_semaphore()

    def greet(place):
        pl.semaphore_signal(barrier, inc=1, device_id=place, device_id_type=MESH)

    greet({"sub": sub + 1 - 2 * bit0, "panel": panel})
    greet({"sub": sub + 2 - 4 * bit1, "panel": panel})

    @pl.when(sub > 0)
    def _():
        greet({"sub": sub - 1, "panel": panel})

    @pl.when(sub < n_sub - 1)
    def _():
        greet({"sub": sub + 1, "panel": panel})

    for step in range(1, n_panel):
        greet({"sub": sub, "panel": lax.rem(panel + step, n_panel)})
    for step in range(1, high):
        greet({"sub": lax.rem(my_high + step, high) * LOW + low, "panel": panel})

    phi_copies = [
        pltpu.make_async_copy(
            phi_hbm.at[:, :, pl.ds(c * width, width)],
            ext[c].at[pl.ds(halo, block_rows)],
            local_sem.at[c],
        )
        for c in range(parts)
    ]
    tile_copy = pltpu.make_async_copy(tiles_hbm, tiles, local_sem.at[parts])
    for copy in phi_copies:
        copy.start()
    tile_copy.start()

    def halo_copy(c, side):
        return pltpu.make_async_remote_copy(
            src_ref=halo_out.at[c, side],
            dst_ref=halo_in.at[c, side],
            send_sem=halo_send.at[c, side],
            recv_sem=halo_recv.at[c, side],
            device_id={"sub": sub + 1 - 2 * side, "panel": panel},
            device_id_type=MESH,
        )

    def prepare_halo(c):
        phi_copies[c].wait()
        for i in range(halo):
            halo_out[c, 0, i] = ext[c][halo + to_right_ref[i]]
            halo_out[c, 1, i] = ext[c][halo + to_left_ref[i]]

    def send_halo(c):
        @pl.when(sub < n_sub - 1)
        def _():
            halo_copy(c, 0).start()

        @pl.when(sub > 0)
        def _():
            halo_copy(c, 1).start()

    prepare_halo(0)
    ends = jnp.where(sub > 0, 1, 0) + jnp.where(sub < n_sub - 1, 1, 0)
    pl.semaphore_wait(barrier, 2 + (n_panel - 1) + (high - 1) + ends)
    send_halo(0)
    for c in range(1, parts):
        prepare_halo(c)

    def panel_copy(step, piece, owner):
        block = lhs.at[owner * per_panel + piece, :, pl.ds(0, mode_rows), :]
        return pltpu.make_async_remote_copy(
            src_ref=block,
            dst_ref=block,
            send_sem=pan_send.at[step, piece],
            recv_sem=pan_recv.at[step, piece],
            device_id={"sub": sub, "panel": lax.rem(panel + step, n_panel)},
            device_id_type=MESH,
        )

    for piece in range(per_panel):

        def transposed(b, carry, piece=piece):
            for q in range(LOW):
                at = (piece * LOW + q) * mode_rows
                lhs[
                    panel * per_panel + piece,
                    q,
                    pl.ds(0, mode_rows),
                    pl.ds(pl.multiple_of(b * tile, tile), tile),
                ] = jnp.transpose(
                    ext[at // width][halo + b, :, pl.ds(at % width, mode_rows)]
                )
            return carry

        lax.fori_loop(0, block_rows, transposed, 0)
        for step in range(1, n_panel):
            panel_copy(step, piece, panel).start()

    listed = rows_ref.shape[1]
    target = owner_ref[...] * IF_DEV + slot_ref[...]
    places = lax.broadcasted_iota(jnp.int32, (n_sub * IF_DEV, listed), 0)
    hit[...] = (places == target).astype(f32).astype(bf16)
    piece_rows = min(512, rows)

    def select(i, carry):
        at = pl.multiple_of(i * piece_rows, piece_rows)
        place = lax.broadcasted_iota(jnp.int32, (piece_rows, listed), 0) + at
        onehot = (place == rows_ref[...]).astype(f32).astype(bf16)
        found = lax.dot_general(
            hit[...],
            onehot,
            (((1,), (1,)), ((), ())),
            preferred_element_type=f32,
        ).astype(bf16)
        lhs[:, :, pl.ds(mode_rows, IF_DEV), pl.ds(at, piece_rows)] = found.reshape(
            high, LOW, IF_DEV, piece_rows
        )
        return carry

    lax.fori_loop(0, rows // piece_rows, select, 0)
    for c in range(parts):
        ext[c][empty] = jnp.zeros((tile, width), bf16)
    tile_copy.wait()

    def products(c):
        for side in range(2):
            there = sub > 0 if side == 0 else sub < n_sub - 1
            place = pl.ds(side * (halo + block_rows), halo)

            @pl.when(there)
            def _(side=side, place=place):
                halo_copy(c, side).wait_recv()
                ext[c][place] = halo_in[c, side]

            @pl.when(jnp.logical_not(there))
            def _(place=place):
                ext[c][place] = jnp.zeros((halo, tile, width), bf16)

        if c + 1 < parts:
            send_halo(c + 1)

        def block_row(b, carry):
            count = counts_ref[0, b]
            left = jnp.concatenate([tiles[b, j] for j in range(slots)], axis=1)
            right = jnp.concatenate(
                [
                    ext[c][jnp.where(j < count, cols_ref[j, b], empty)]
                    for j in range(slots)
                ],
                axis=0,
            )
            kphi[c, pl.ds(pl.multiple_of(b * tile, tile), tile), :] = jnp.dot(
                left, right, preferred_element_type=f32
            ).astype(bf16)
            return carry

        lax.fori_loop(0, block_rows, block_row, 0, unroll=4)

    def first_copy(k):
        return pltpu.make_async_remote_copy(
            src_ref=s1_out.at[k],
            dst_ref=s1_in.at[k],
            send_sem=s1_send.at[k],
            recv_sem=s1_recv.at[k],
            device_id={"sub": order(first_of(k))[4], "panel": panel},
            device_id_type=MESH,
        )

    def second_copy(k):
        return pltpu.make_async_remote_copy(
            src_ref=s2_out.at[k],
            dst_ref=s2_in.at[k],
            send_sem=s2_send.at[k],
            recv_sem=s2_recv.at[k],
            device_id={"sub": order(first_of(k))[5], "panel": panel},
            device_id_type=MESH,
        )

    def third_copy(k, h, slot):
        return pltpu.make_async_remote_copy(
            src_ref=z_out.at[k],
            dst_ref=z_in.at[slot],
            send_sem=z_send.at[k],
            recv_sem=z_recv.at[slot],
            device_id={"sub": h * LOW + low, "panel": panel},
            device_id_type=MESH,
        )

    def cross_copy(stage, k, place):
        out, into, send, recv = (
            (b1_out, b1_in, b1_send, b1_recv),
            (b2_out, b2_in, b2_send, b2_recv),
            (b3_out, b3_in, b3_send, b3_recv),
            (b4_out, b4_in, b4_send, b4_recv),
        )[stage]
        return pltpu.make_async_remote_copy(
            src_ref=out.at[k],
            dst_ref=into.at[k],
            send_sem=send.at[k],
            recv_sem=recv.at[k],
            device_id={"sub": place, "panel": panel},
            device_id_type=MESH,
        )

    def cross_near(k):
        return cross_copy(0, k, flip(1) * LOW + low)

    def cross_far(c):
        return cross_copy(1, c, flip(2) * LOW + low)

    def cross_first(c):
        return cross_copy(2, c, order(1 - odd)[4])

    def cross_second(c):
        return cross_copy(3, c, order(1 - odd)[5])

    head, tail = pl.ds(0, direct), pl.ds(direct, cross)

    def cross_send(k):
        c = k // high
        at = 2 * c + mask_of(k) // 2
        b1_out[at] = part[k, :, tail, :].astype(bf16)
        cross_near(at).start()

    def cross_pass(k):
        c = k // high
        cross_near(2 * c + 1).wait_recv()
        b2_out[c] = (part[k, :, tail, :] + b1_in[2 * c + 1].astype(f32)).astype(bf16)
        cross_far(c).start()

    def cross_own(k):
        c = k // high
        cross_near(2 * c).wait_recv()
        cross_far(c).wait_recv()
        part[k, :, tail, :] += b1_in[2 * c].astype(f32) + b2_in[c].astype(f32)
        first_bit, _, first_weight, second_weight, _, _ = order(1 - odd)
        for j in range(2):
            q = (1 - first_bit) * first_weight + j * second_weight
            b3_out[c, j] = part[k, q, tail, :].astype(bf16)
        cross_first(c).start()

    def cross_turn(k):
        c = k // high
        first_bit, second_bit, first_weight, second_weight, _, _ = order(1 - odd)
        cross_first(c).wait_recv()
        q = first_bit * first_weight + (1 - second_bit) * second_weight
        b4_out[c] = (
            part[k, q, tail, :] + b3_in[c, 1 - second_bit].astype(f32)
        ).astype(bf16)
        cross_second(c).start()

    def put(value, start, at):
        count = value.shape[0]
        cut = max(0, min(count, mode_rows - start))
        if cut:
            red_ref[pl.ds(start, cut), at] = value[:cut]
        if cut < count:
            load_ref[pl.ds(start + cut - mode_rows, count - cut), at] = value[cut:]

    def columns_of(c):
        return pl.ds(pl.multiple_of(c * width, width), width)

    def cross_last(k):
        c = k // high
        _, second_bit, _, _, _, _ = order(1 - odd)
        cross_second(c).wait_recv()
        put(
            part[k, low, tail, :]
            + b3_in[c, second_bit].astype(f32)
            + b4_in[c].astype(f32),
            direct,
            columns_of(c),
        )

    def gathered(c):
        at = columns_of(c)
        cut = min(direct, mode_rows)

        def one(i, inner):
            slot = c * high + lax.rem(my_high + 1 + i, high)
            third_copy(slot, my_high, slot).wait_recv()
            red_ref[pl.ds(0, cut), at] += z_in[slot, pl.ds(0, cut), :].astype(f32)
            if direct > mode_rows:
                extra = pl.ds(0, direct - mode_rows)
                load_ref[extra, at] += z_in[slot, pl.ds(cut, direct - cut), :].astype(f32)
            return inner

        lax.fori_loop(0, high - 1, one, 0)

    def step_of(t, carry):
        for c in range(parts):

            @pl.when(t == c * high)
            def _(c=c):
                products(c)

        for step in range(1, n_panel):

            @pl.when(t == step * per_panel)
            def _(step=step):
                owner = lax.rem(panel + step, n_panel)
                for piece in range(per_panel):
                    panel_copy(n_panel - step, piece, owner).wait_recv()

        @pl.when(t < total_steps)
        def _():
            c, h = t // high, dest(t)
            first_bit, _, first_weight, second_weight, _, _ = order(first_of(t))
            product = jnp.dot(
                lhs[h].reshape(LOW * out_rows, rows),
                kphi[c],
                preferred_element_type=f32,
            )
            part[t] = product.reshape(LOW, out_rows, width)
            for j in range(2):
                q = (1 - first_bit) * first_weight + j * second_weight
                s1_out[t, j] = part[t, q, head, :].astype(bf16)
            first_copy(t).start()
            if cross:

                @pl.when(lax.rem(mask_of(t), 2) == 1)
                def _():
                    cross_send(t)

        @pl.when((t >= LAG) & (t < total_steps + LAG))
        def _():
            k = t - LAG
            first_bit, second_bit, first_weight, second_weight, _, _ = order(first_of(k))
            first_copy(k).wait_recv()
            q = first_bit * first_weight + (1 - second_bit) * second_weight
            s2_out[k] = (
                part[k, q, head, :] + s1_in[k, 1 - second_bit].astype(f32)
            ).astype(bf16)
            second_copy(k).start()

        @pl.when((t >= NEXT) & (t < total_steps + NEXT))
        def _():
            k = t - NEXT
            c, h = k // high, dest(k)
            _, second_bit, _, _, _, _ = order(first_of(k))
            second_copy(k).wait_recv()
            total = (
                part[k, low, head, :]
                + s1_in[k, second_bit].astype(f32)
                + s2_in[k].astype(f32)
            )

            @pl.when(h != my_high)
            def _():
                z_out[k] = total.astype(bf16)
                third_copy(k, h, c * high + my_high).start()

            @pl.when(h == my_high)
            def _():
                put(total, 0, columns_of(c))

        if cross:
            for wait, mask, action in zip(
                TURNS, (2, 0, 0, 0), (cross_pass, cross_own, cross_turn, cross_last)
            ):
                k = t - wait

                @pl.when((k >= 0) & (k < total_steps) & (mask_of(jnp.maximum(k, 0)) == mask))
                def _(k=k, action=action):
                    action(k)

        done = t - NEXT - REST - (high - 1)

        @pl.when((done >= 0) & (lax.rem(jnp.maximum(done, 0), high) == 0))
        def _():
            gathered(done // high)

        return carry

    last = max(NEXT + REST, TURNS[-1] if cross else 0)
    lax.fori_loop(0, total_steps + last, step_of, 0)

    def drained(k, carry):
        first_copy(k).wait_send()
        second_copy(k).wait_send()

        @pl.when(dest(k) != my_high)
        def _():
            third_copy(k, my_high, k).wait_send()

        return carry

    lax.fori_loop(0, total_steps, drained, 0)
    for c in range(parts):
        if cross:
            cross_near(2 * c).wait_send()
            cross_near(2 * c + 1).wait_send()
            cross_far(c).wait_send()
            cross_first(c).wait_send()
            cross_second(c).wait_send()

        @pl.when(sub < n_sub - 1)
        def _(c=c):
            halo_copy(c, 0).wait_send()

        @pl.when(sub > 0)
        def _(c=c):
            halo_copy(c, 1).wait_send()

    for step in range(1, n_panel):
        for piece in range(per_panel):
            panel_copy(step, piece, panel).wait_send()


def hand_over(red_in, load_in, red_out, load_out):
    red_out[...] = red_in[...]
    load_out[...] = load_in[...]


def body(
    n_sub,
    n_panel,
    stiffness_tiles,
    tile_columns,
    tile_counts,
    phi_modes,
    halo_to_right,
    halo_to_left,
    liner_rows,
    liner_owner,
    liner_slot,
):
    block_rows, slots, tile, _ = stiffness_tiles.shape
    rows, columns = phi_modes.shape
    mode_rows = columns * n_panel // n_sub
    parts, width, high, cross = sizes(n_sub, n_panel, columns)
    out_rows = mode_rows + IF_DEV
    direct = out_rows - cross
    over = cross or 16
    halo = halo_to_right.shape[0]
    listed = liner_rows.shape[0]
    steps = parts * high
    bf16, f32 = jnp.bfloat16, jnp.float32
    smem = pl.BlockSpec(memory_space=pltpu.SMEM)
    vmem = pl.BlockSpec(memory_space=pltpu.VMEM)
    hbm = pl.BlockSpec(memory_space=pl.ANY)
    dma = pltpu.SemaphoreType.DMA
    sums = pl.pallas_call(
        functools.partial(kernel, n_sub, n_panel, parts, cross),
        out_shape=(
            jax.ShapeDtypeStruct((mode_rows, columns), f32),
            jax.ShapeDtypeStruct((IF_DEV, columns), f32),
        ),
        in_specs=[smem, smem, smem, smem, vmem, vmem, vmem, hbm, hbm],
        out_specs=(vmem, vmem),
        scratch_shapes=[
            pltpu.VMEM((block_rows + 2 * halo + 1, tile, width), bf16)
            for _ in range(parts)
        ]
        + [
            pltpu.VMEM((block_rows, slots, tile, tile), bf16),
            pltpu.VMEM((n_sub * IF_DEV, listed), bf16),
            pltpu.VMEM((high, LOW, out_rows, rows), bf16),
            pltpu.VMEM((parts, rows, width), bf16),
            pltpu.VMEM((steps, LOW, out_rows, width), f32),
            pltpu.VMEM((parts, 2, halo, tile, width), bf16),
            pltpu.VMEM((parts, 2, halo, tile, width), bf16),
            pltpu.VMEM((steps, 2, direct, width), bf16),
            pltpu.VMEM((steps, 2, direct, width), bf16),
            pltpu.VMEM((steps, direct, width), bf16),
            pltpu.VMEM((steps, direct, width), bf16),
            pltpu.VMEM((steps, direct, width), bf16),
            pltpu.VMEM((steps, direct, width), bf16),
            pltpu.VMEM((2 * parts, LOW, over, width), bf16),
            pltpu.VMEM((2 * parts, LOW, over, width), bf16),
            pltpu.VMEM((parts, LOW, over, width), bf16),
            pltpu.VMEM((parts, LOW, over, width), bf16),
            pltpu.VMEM((parts, 2, over, width), bf16),
            pltpu.VMEM((parts, 2, over, width), bf16),
            pltpu.VMEM((parts, over, width), bf16),
            pltpu.VMEM((parts, over, width), bf16),
            dma((parts + 1,)),
            dma((parts, 2)),
            dma((parts, 2)),
            dma((n_panel, high // n_panel)),
            dma((n_panel, high // n_panel)),
        ]
        + [dma((steps,))] * 6
        + [dma((2 * parts,))] * 2
        + [dma((parts,))] * 6,
        compiler_params=pltpu.CompilerParams(
            collective_id=0, has_side_effects=True, vmem_limit_bytes=60 << 20
        ),
    )(
        tile_columns.T,
        tile_counts,
        halo_to_right,
        halo_to_left,
        liner_rows.reshape(1, listed),
        liner_owner.reshape(1, listed),
        liner_slot.reshape(1, listed),
        stiffness_tiles,
        phi_modes.reshape(block_rows, tile, columns),
    )
    return pl.pallas_call(
        hand_over,
        out_shape=tuple(jax.ShapeDtypeStruct(x.shape, f32) for x in sums),
        in_specs=[vmem, vmem],
        out_specs=(vmem, vmem),
    )(*sums)


def solution(mesh):
    return jax.shard_map(
        functools.partial(body, mesh.shape["sub"], mesh.shape["panel"]),
        mesh=mesh,
        in_specs=(
            P("sub", None, None, None),
            P("sub", None),
            P("sub", None),
            P("sub", "panel"),
            P("sub"),
            P("sub"),
            P("sub"),
            P("sub", None),
            P("sub"),
        ),
        out_specs=(P("sub", "panel"), P("sub", "panel")),
        check_vma=False,
    )
```

time: 93.5 us -> 76.4 us (0.82)
  Pallas kernels: 89.2 us -> 75.2 us
  local copies, waits for them, and re-layouts: 3.45 us -> 0 us
    pallas_call x1 -> x2, Pallas kernels: 89.2 us -> 75.2 us  [the longest x1 73.3 us: body(): pl.pallas_call(functools.partial(kernel, n_sub, n_panel, parts, cross), o...]
    unnamed x2 -> x0, local copies, waits for them, and re-layouts: 3.45 us -> none
where the time goes in v2:
time: 76.4 us; the launch traced here: 75.9 us
  Pallas kernels  75.2 us (98%)
    pallas_call x1, Pallas kernels, body(): pl.pallas_call(functools.partial(kernel, n_sub, n_panel, parts, cross), o...  73.3 us
    pallas_call x1, Pallas kernels, body(): pl.pallas_call(hand_over, out_shape=tuple((jax.ShapeDtypeStruct(x.shape,...  1.93 us

profile of v2, /device:TPU:0, one launch (start us, length us, event | category | flops | bytes accessed | tf_op | source)
XLA Modules:
  0.0 75.9 jit_solution(1111545629471976603)
XLA Ops:
  0.6 73.3 %shard_map.104 = (f32[128,1024]{1,0:T(8,128)}, f32[32,1024]{1,0:T(8,128)}) custom-call(s32[8,16]{1,0:T(8,128)} %bitcast.6, s32[1,16]{1,0:T(1,128)} %refs_1_.1, s32[2]{0:T(128)} %refs_2_.1, s32[2]{0:T(128)} %refs_3_.1, s32[1,512]{1,0:T(1,128)} %bitcast.7, s32[1,512]{1,0:T(1,128)} %bitcast.8, s32[1,512]{1,0:T(1,128)} %bitcast.9, ...), custom_call_target="tpu_custom_call" | custom-call | tf_op jit(solution)/shard_map/pallas_call | solution.py:535
  73.9 1.9 %shard_map.105 = (f32[128,1024]{1,0:T(8,128)}, f32[32,1024]{1,0:T(8,128)}) custom-call(f32[128,1024]{1,0:T(8,128)} %get-tuple-element.4.red_in, f32[32,1024]{1,0:T(8,128)} %get-tuple-element.5.load_in), custom_call_target="tpu_custom_call" | custom-call | tf_op jit(solution)/shard_map/pallas_call | solution.py:592

commit v3 on v2

--- a/solution.py
+++ b/solution.py
@@ -10,9 +10,9 @@
 IF_DEV = 32
 LOW = 4
 LAG = 3
-NEXT = 5
+NEXT = 7
 REST = 3
-TURNS = (1, 3, 6, 8)
+TURNS = (1, 3, 7, 10)
 CROSS_ROWS = 48
 MESH = pl.DeviceIdType.MESH
 
@@ -83,7 +83,7 @@
         k = lax.rem(t, high)
         apart = jnp.abs(high1 - panel)
         begin = 2 * jnp.abs(k // 2 - apart) + 1 - lax.rem(k, 2)
-        later = 3 - k // 2 - 2 * lax.rem(k, 2)
+        later = 3 - k
         return jnp.where(t < high, begin, later)
 
     def dest(t):

time: 76.4 us -> 72.3 us (0.946)
  Pallas kernels: 75.2 us -> 71.5 us
    pallas_call x1, Pallas kernels: 73.3 us -> 69.6 us  [body(): pl.pallas_call(functools.partial(kernel, n_sub, n_panel, parts, cross), o...]
where the time goes in v3:
time: 72.3 us; the launch traced here: 72.1 us
  Pallas kernels  71.5 us (99%)
    pallas_call x1, Pallas kernels, body(): pl.pallas_call(functools.partial(kernel, n_sub, n_panel, parts, cross), o...  69.6 us
    pallas_call x1, Pallas kernels, body(): pl.pallas_call(hand_over, out_shape=tuple((jax.ShapeDtypeStruct(x.shape,...  1.93 us

profile of v3, /device:TPU:0, one launch (start us, length us, event | category | flops | bytes accessed | tf_op | source)
XLA Modules:
  0.0 72.1 jit_solution(11419238009933605288)
XLA Ops:
  0.6 69.6 %shard_map.104 = (f32[128,1024]{1,0:T(8,128)}, f32[32,1024]{1,0:T(8,128)}) custom-call(s32[8,16]{1,0:T(8,128)} %bitcast.6, s32[1,16]{1,0:T(1,128)} %refs_1_.1, s32[2]{0:T(128)} %refs_2_.1, s32[2]{0:T(128)} %refs_3_.1, s32[1,512]{1,0:T(1,128)} %bitcast.7, s32[1,512]{1,0:T(1,128)} %bitcast.8, s32[1,512]{1,0:T(1,128)} %bitcast.9, ...), custom_call_target="tpu_custom_call" | custom-call | tf_op jit(solution)/shard_map/pallas_call | solution.py:535
  70.2 1.9 %shard_map.105 = (f32[128,1024]{1,0:T(8,128)}, f32[32,1024]{1,0:T(8,128)}) custom-call(f32[128,1024]{1,0:T(8,128)} %get-tuple-element.4.red_in, f32[32,1024]{1,0:T(8,128)} %get-tuple-element.5.load_in), custom_call_target="tpu_custom_call" | custom-call | tf_op jit(solution)/shard_map/pallas_call | solution.py:592

commit v4 on v3

--- a/solution.py
+++ b/solution.py
@@ -11,7 +11,7 @@
 LOW = 4
 LAG = 3
 NEXT = 7
-REST = 3
+REST = 4
 TURNS = (1, 3, 7, 10)
 CROSS_ROWS = 48
 MESH = pl.DeviceIdType.MESH
@@ -152,6 +152,10 @@
             halo_copy(c, 1).start()
 
     prepare_halo(0)
+    listed = rows_ref.shape[1]
+    target = owner_ref[...] * IF_DEV + slot_ref[...]
+    places = lax.broadcasted_iota(jnp.int32, (n_sub * IF_DEV, listed), 0)
+    hit[...] = (places == target).astype(f32).astype(bf16)
     ends = jnp.where(sub > 0, 1, 0) + jnp.where(sub < n_sub - 1, 1, 0)
     pl.semaphore_wait(barrier, 2 + (n_panel - 1) + (high - 1) + ends)
     send_halo(0)
@@ -188,10 +192,6 @@
         for step in range(1, n_panel):
             panel_copy(step, piece, panel).start()
 
-    listed = rows_ref.shape[1]
-    target = owner_ref[...] * IF_DEV + slot_ref[...]
-    places = lax.broadcasted_iota(jnp.int32, (n_sub * IF_DEV, listed), 0)
-    hit[...] = (places == target).astype(f32).astype(bf16)
     piece_rows = min(512, rows)
 
     def select(i, carry):
@@ -330,6 +330,8 @@
             q = (1 - first_bit) * first_weight + j * second_weight
             b3_out[c, j] = part[k, q, tail, :].astype(bf16)
         cross_first(c).start()
+        cross_near(2 * c).wait_send()
+        cross_near(2 * c + 1).wait_send()
 
     def cross_turn(k):
         c = k // high
@@ -340,6 +342,7 @@
             part[k, q, tail, :] + b3_in[c, 1 - second_bit].astype(f32)
         ).astype(bf16)
         cross_second(c).start()
+        cross_far(c).wait_send()
 
     def put(value, start, at):
         count = value.shape[0]
@@ -356,6 +359,7 @@
         c = k // high
         _, second_bit, _, _, _, _ = order(1 - odd)
         cross_second(c).wait_recv()
+        cross_first(c).wait_send()
         put(
             part[k, low, tail, :]
             + b3_in[c, second_bit].astype(f32)
@@ -378,6 +382,15 @@
             return inner
 
         lax.fori_loop(0, high - 1, one, 0)
+
+        def sent(k, inner):
+            @pl.when(dest(k) != my_high)
+            def _():
+                third_copy(k, my_high, k).wait_send()
+
+            return inner
+
+        lax.fori_loop(c * high, (c + 1) * high, sent, 0)
 
     def step_of(t, carry):
         for c in range(parts):
@@ -424,6 +437,7 @@
                 part[k, q, head, :] + s1_in[k, 1 - second_bit].astype(f32)
             ).astype(bf16)
             second_copy(k).start()
+            first_copy(k).wait_send()
 
         @pl.when((t >= NEXT) & (t < total_steps + NEXT))
         def _():
@@ -446,6 +460,8 @@
             def _():
                 put(total, 0, columns_of(c))
 
+            second_copy(k).wait_send()
+
         if cross:
             for wait, mask, action in zip(
                 TURNS, (2, 0, 0, 0), (cross_pass, cross_own, cross_turn, cross_last)
@@ -467,23 +483,8 @@
     last = max(NEXT + REST, TURNS[-1] if cross else 0)
     lax.fori_loop(0, total_steps + last, step_of, 0)
 
-    def drained(k, carry):
-        first_copy(k).wait_send()
-        second_copy(k).wait_send()
-
-        @pl.when(dest(k) != my_high)
-        def _():
-            third_copy(k, my_high, k).wait_send()
-
-        return carry
-
-    lax.fori_loop(0, total_steps, drained, 0)
     for c in range(parts):
         if cross:
-            cross_near(2 * c).wait_send()
-            cross_near(2 * c + 1).wait_send()
-            cross_far(c).wait_send()
-            cross_first(c).wait_send()
             cross_second(c).wait_send()
 
         @pl.when(sub < n_sub - 1)

time: 72.3 us -> 71.9 us (level)
  no operation moved by 1% of the time
where the time goes in v4:
time: 71.9 us; the launch traced here: 71.7 us
  Pallas kernels  71 us (99%)
    pallas_call x1, Pallas kernels, body(): pl.pallas_call(functools.partial(kernel, n_sub, n_panel, parts, cross), o...  69.1 us
    pallas_call x1, Pallas kernels, body(): pl.pallas_call(hand_over, out_shape=tuple((jax.ShapeDtypeStruct(x.shape,...  1.93 us

profile of v4, /device:TPU:0, one launch (start us, length us, event | category | flops | bytes accessed | tf_op | source)
XLA Modules:
  0.0 71.7 jit_solution(2079943127723994725)
XLA Ops:
  0.6 69.1 %shard_map.104 = (f32[128,1024]{1,0:T(8,128)}, f32[32,1024]{1,0:T(8,128)}) custom-call(s32[8,16]{1,0:T(8,128)} %bitcast.6, s32[1,16]{1,0:T(1,128)} %refs_1_.1, s32[2]{0:T(128)} %refs_2_.1, s32[2]{0:T(128)} %refs_3_.1, s32[1,512]{1,0:T(1,128)} %bitcast.7, s32[1,512]{1,0:T(1,128)} %bitcast.8, s32[1,512]{1,0:T(1,128)} %bitcast.9, ...), custom_call_target="tpu_custom_call" | custom-call | tf_op jit(solution)/shard_map/pallas_call | solution.py:536
  69.8 1.9 %shard_map.105 = (f32[128,1024]{1,0:T(8,128)}, f32[32,1024]{1,0:T(8,128)}) custom-call(f32[128,1024]{1,0:T(8,128)} %get-tuple-element.4.red_in, f32[32,1024]{1,0:T(8,128)} %get-tuple-element.5.load_in), custom_call_target="tpu_custom_call" | custom-call | tf_op jit(solution)/shard_map/pallas_call | solution.py:593

commit v5 on v4

--- a/solution.py
+++ b/solution.py
@@ -246,7 +246,7 @@
             ).astype(bf16)
             return carry
 
-        lax.fori_loop(0, block_rows, block_row, 0, unroll=4)
+        lax.fori_loop(0, block_rows, block_row, 0, unroll=16)
 
     def first_copy(k):
         return pltpu.make_async_remote_copy(

time: 71.9 us -> 72.4 us (level)
  no operation moved by 1% of the time
where the time goes in v5:
time: 72.4 us; the launch traced here: 72.2 us
  Pallas kernels  71.6 us (99%)
    pallas_call x1, Pallas kernels, body(): pl.pallas_call(functools.partial(kernel, n_sub, n_panel, parts, cross), o...  69.6 us
    pallas_call x1, Pallas kernels, body(): pl.pallas_call(hand_over, out_shape=tuple((jax.ShapeDtypeStruct(x.shape,...  1.93 us

profile of v5, /device:TPU:0, one launch (start us, length us, event | category | flops | bytes accessed | tf_op | source)
XLA Modules:
  0.0 72.2 jit_solution(15042304600683805141)
XLA Ops:
  0.6 69.6 %shard_map.104 = (f32[128,1024]{1,0:T(8,128)}, f32[32,1024]{1,0:T(8,128)}) custom-call(s32[8,16]{1,0:T(8,128)} %bitcast.6, s32[1,16]{1,0:T(1,128)} %refs_1_.1, s32[2]{0:T(128)} %refs_2_.1, s32[2]{0:T(128)} %refs_3_.1, s32[1,512]{1,0:T(1,128)} %bitcast.7, s32[1,512]{1,0:T(1,128)} %bitcast.8, s32[1,512]{1,0:T(1,128)} %bitcast.9, ...), custom_call_target="tpu_custom_call" | custom-call | tf_op jit(solution)/shard_map/pallas_call | solution.py:536
  70.3 1.9 %shard_map.105 = (f32[128,1024]{1,0:T(8,128)}, f32[32,1024]{1,0:T(8,128)}) custom-call(f32[128,1024]{1,0:T(8,128)} %get-tuple-element.4.red_in, f32[32,1024]{1,0:T(8,128)} %get-tuple-element.5.load_in), custom_call_target="tpu_custom_call" | custom-call | tf_op jit(solution)/shard_map/pallas_call | solution.py:593
